TPU v7x, 512 devices: a whole 4x8x8 slice. The times are simulated.
512 devices in a mesh: shard: 128 (over y, z, core), blk: 4 (over x).
Axes of the slice: x: 4, y: 8, z: 8, core: 2. Of those that a mesh axis runs over, the one named last changes fastest.
Arguments:
- queries: bfloat16 [256, 32, 128], P('shard'), may hold values from -0.5 to 0.5
- passages: bfloat16 [8192, 128, 128], P('shard', 'blk'), may hold values from -0.5 to 0.5
- lengths: int32 [8192], P('shard'), may hold values from 16 to 128, as said below
- pair_query: int32 [16384, 12], P('shard'), may hold values from 0 to 1
- pair_passage: int32 [16384, 12], P('shard'), may hold values from 0 to 63
- send_counts: int32 [16384], P('shard'), may hold values from 1 to 12, as said below
Outputs:
- pair_scores: float32 [16384, 12], P('shard')
Inputs may be any that keep to these rules, and one draw needn't show every extreme that they name: `lengths`: every passage has at least 16 tokens; some passage has exactly 128. `send_counts`: every route has at least one live slot; in every draw one passage owner receives 12 live pairs from every query owner.
All inputs are finite; a program needn't handle non-finite values.
Results may differ from a plain program's by a relative error of at most 0.0003.
Values may be sent and summed in bfloat16 or wider, within the bound.
A program may use at most 64 MiB of HBM per device.

v0:
```python
import math

import jax
import jax.numpy as jnp
from jax import lax
from jax.sharding import PartitionSpec as P


def block_maxima(query_tile_rows, passage_idx, passages, lengths, offset):
    token_vectors = jnp.take(passages, passage_idx, axis=0)
    match_scores = jnp.einsum(
        "oer,ogr->oeg", query_tile_rows, token_vectors, preferred_element_type=jnp.float32
    )
    positions = offset + jnp.arange(token_vectors.shape[1], dtype=jnp.int32)
    live = positions[None, :] < jnp.take(lengths, passage_idx)[:, None]
    match_scores = jnp.where(live[:, None, :], match_scores, -1e30)
    return jnp.max(match_scores, axis=2)


def local(queries, passages, lengths, pair_query, pair_passage, send_counts):
    owners = lax.axis_size("shard")
    q_local = queries.shape[0]
    slots = pair_query.shape[1]
    q_tokens = queries.shape[1]
    embed = queries.shape[2]
    offset = lax.axis_index("blk") * passages.shape[1]
    global_query = pair_query + lax.axis_index("shard") * q_local
    forwarded_rows = lax.all_to_all(
        jnp.stack([global_query, pair_passage], axis=2),
        "shard",
        split_axis=0,
        concat_axis=0,
        tiled=True,
    )
    total = owners * slots
    width = math.gcd(total, 128)
    passage_ids = forwarded_rows[:, :, 1].reshape(-1, width)
    rows = jnp.take(queries, pair_query.reshape(-1), axis=0).reshape(owners, slots, q_tokens, embed)
    arrived = lax.all_to_all(rows, "shard", split_axis=0, concat_axis=0, tiled=True)
    arrived = arrived.reshape(-1, width, q_tokens, embed)

    def score_rows(items):
        query_tile_rows, passage_idx = items
        return block_maxima(query_tile_rows, passage_idx, passages, lengths, offset)

    maxima = lax.map(score_rows, (arrived, passage_ids))
    maxima = maxima.reshape(total, q_tokens)
    maxima = lax.pmax(maxima, "blk")
    totals = jnp.sum(maxima, axis=1).reshape(owners, slots)
    returned = lax.all_to_all(totals, "shard", split_axis=0, concat_axis=0, tiled=True)
    valid = jnp.arange(slots, dtype=jnp.int32)[None, :] < send_counts[:, None]
    return jnp.where(valid, returned, 0.0)


def solution(mesh):
    placed = (
        P("shard", None, None),
        P("shard", "blk", None),
        P("shard"),
        P("shard", None),
        P("shard", None),
        P("shard"),
    )
    return jax.shard_map(
        local, mesh=mesh, in_specs=placed, out_specs=P("shard", None), check_vma=False
    )
```

profile of v0, /device:TPU:1, one launch (start us, length us, event | category | flops | bytes accessed | tf_op | source)
XLA Modules:
  0.0 621.7 jit_solution(2284634721329277477)
XLA Ops:
  6.5 0.7 broadcast_add_fusion
  7.3 0.7 stack.10
  8.0 0.8 copy.19
  8.7 18.4 %all-to-all-start = ((s32[128,12,2]{1,2,0:T(2,128)}), s32[128,12,2]{1,2,0:T(2,128)S(1)}, u32[]{:S(2)}, u32[]{:S(2)}) async-start(s32[128,12,2]{1,2,0:T(2,128)} %copy.19), calls=%async_computation | async-start | bytes 262144 | tf_op jit(solution)/shard_map/all_to_all | solution.py:28
  27.2 0.8 copy.21
  28.0 0.7 compare_and_fusion.1
  29.0 7.4 %gather_fusion.2 = bf16[1536,32,128]{2,1,0:T(8,128)(2,1)} fusion(bf16[2,32,128]{2,1,0:T(8,128)(2,1)S(1)} %copy-done, s32[2048]{0:T(1024)S(1)} %pad_clamp_fusion.1), kind=kCustom, calls=%fused_computation.2 | custom fusion | bytes 25171968 | tf_op jit(solution)/shard_map/jit(_take)/gather | solution.py:38
  36.3 11.0 %broadcast_select_fusion.1 = bf16[128,12,32,128]{3,2,1,0:T(8,128)(2,1)} fusion(bf16[128,12,32,128]{3,2,1,0:T(8,128)(2,1)} %bitcast.29, pred[128,12]{1,0:T(8,128)(4,1)S(1)} %copy.20), kind=kLoop, calls=%fused_computation.21 | loop fusion | flops 6291456 | bytes 25167360 | tf_op jit(solution)/shard_map/jit(_take)/select_n | solution.py:38
  47.3 14.3 %all-to-all-start.1 = ((bf16[128,12,32,128]{3,2,1,0:T(8,128)(2,1)}), bf16[128,12,32,128]{3,2,1,0:T(8,128)(2,1)}, u32[]{:S(2)}, u32[]{:S(2)}) async-start(bf16[128,12,32,128]{3,2,1,0:T(8,128)(2,1)} %broadcast_select_fusion.1), calls=%async_computation.1 | async-start | bytes 25165824 | tf_op jit(solution)/shard_map/all_to_all | solution.py:39
  61.7 0.2 slice_reduce_fusion
  62.0 365.8 %all-to-all-done.1 = bf16[128,12,32,128]{3,2,1,0:T(8,128)(2,1)} async-done(((bf16[128,12,32,128]{3,2,1,0:T(8,128)(2,1)}), bf16[128,12,32,128]{3,2,1,0:T(8,128)(2,1)}, u32[]{:S(2)}, u32[]{:S(2)}) %all-to-all-start.1) | async-done | bytes 12582944 | tf_op jit(solution)/shard_map/all_to_all | solution.py:39
  427.8 59.2 %while.10 = (s32[]{:T(128)}, f32[12,128,32]{2,1,0:T(8,128)}, s32[]{:T(128)}, s32[12,128]{1,0:T(8,128)S(1)}, s32[64]{0:T(128)S(1)}, /*index=5*/bf16[12,128,32,128...) while((s32[]{:T(128)}, f32[12,128,32]{2,1,0:T(8,128)}, s32[]{:T(128)}, s32[12,128]{1,0:T(8,128)S(1)}, ...), condition=%wide.region_2.3_spmd, body=%wide.region_0.0_spmd.sunk | while | flops 34343200 | bytes 4312161 | solution.py:46
  427.9 1.2 gather_fusion.1
  429.2 0.8 gather_fusion
  430.0 2.2 select_reduce_fusion.2
  432.2 0.6 bitcast_dynamic-update-slice_fusion.2
  432.8 1.2 gather_fusion.1
  434.2 0.8 gather_fusion
  434.9 2.2 select_reduce_fusion.2
  437.1 0.6 bitcast_dynamic-update-slice_fusion.2
  437.8 1.2 gather_fusion.1
  439.1 0.8 gather_fusion
  439.9 2.2 select_reduce_fusion.2
  442.0 0.6 bitcast_dynamic-update-slice_fusion.2
  442.7 1.2 gather_fusion.1
  444.0 0.8 gather_fusion
  444.8 2.2 select_reduce_fusion.2
  447.0 0.6 bitcast_dynamic-update-slice_fusion.2
  447.6 1.2 gather_fusion.1
  449.0 0.8 gather_fusion
  449.7 2.2 select_reduce_fusion.2
  451.9 0.6 bitcast_dynamic-update-slice_fusion.2
  452.6 1.2 gather_fusion.1
  453.9 0.8 gather_fusion
  454.7 2.2 select_reduce_fusion.2
  456.8 0.6 bitcast_dynamic-update-slice_fusion.2
  457.5 1.2 gather_fusion.1
  458.8 0.8 gather_fusion
  459.6 2.2 select_reduce_fusion.2
  461.8 0.6 bitcast_dynamic-update-slice_fusion.2
  462.4 1.2 gather_fusion.1
  463.8 0.8 gather_fusion
  464.6 2.2 select_reduce_fusion.2
  466.7 0.6 bitcast_dynamic-update-slice_fusion.2
  467.4 1.2 gather_fusion.1
  468.7 0.8 gather_fusion
  469.5 2.2 select_reduce_fusion.2
  471.7 0.6 bitcast_dynamic-update-slice_fusion.2
  472.3 1.2 gather_fusion.1
  473.7 0.8 gather_fusion
  474.4 2.2 select_reduce_fusion.2
  476.6 0.6 bitcast_dynamic-update-slice_fusion.2
  477.2 1.2 gather_fusion.1
  478.6 0.8 gather_fusion
  479.4 2.2 select_reduce_fusion.2
  481.5 0.6 bitcast_dynamic-update-slice_fusion.2
  482.2 1.2 gather_fusion.1
  483.5 0.8 gather_fusion
  484.3 2.2 select_reduce_fusion.2
  486.5 0.6 bitcast_dynamic-update-slice_fusion.2
  487.1 98.1 %all-reduce.2.cloned.1.call-done = f32[1536,32]{1,0:T(8,128)} async-done(((f32[1536,32]{1,0:T(8,128)}), f32[1536,32]{1,0:T(8,128)}) %all-reduce.2.cloned.1.call-update) | async-done | bytes 196624 | tf_op jit(solution)/shard_map/pmax | solution.py:48
  585.2 1.4 reduce_sum.9
  586.7 27.4 %all_to_all.22 = f32[128,1,12]{2,1,0:T(1,128)S(1)} all-to-all(f32[128,1,12]{2,1,0:T(1,128)S(1)} %bitcast.31), channel_id=1, replica_groups=mesh['shard'=128,'blk'=4] {'shard'}, dimensions={0} | all-to-all | bytes 12288 | tf_op jit(solution)/shard_map/all_to_all | solution.py:50
  614.2 0.7 copy.23
  (81 shorter events, 2.1 us)
Async XLA Ops:
  6.5 22.4 %copy-start = (bf16[2,32,128]{2,1,0:T(8,128)(2,1)S(1)}, bf16[2,32,128]{2,1,0:T(8,128)(2,1)}, u32[]{:S(2)}) copy-start(bf16[2,32,128]{2,1,0:T(8,128)(2,1)} %param.8) | copy-start | bytes 49156
  8.7 38.6 %all-to-all-start = ((s32[128,12,2]{1,2,0:T(2,128)}), s32[128,12,2]{1,2,0:T(2,128)S(1)}, u32[]{:S(2)}, u32[]{:S(2)}) async-start(s32[128,12,2]{1,2,0:T(2,128)} %copy.19), calls=%async_computation | async-start | bytes 262144 | tf_op jit(solution)/shard_map/all_to_all | solution.py:28
  47.3 380.5 %copy-start.1 = (s32[64]{0:T(128)S(1)}, s32[64]{0:T(128)}, u32[]{:S(2)}) copy-start(s32[64]{0:T(128)} %param.10) | copy-start | bytes 772
  47.3 380.5 %copy-start.2 = (bf16[64,32,128]{2,1,0:T(8,128)(2,1)S(1)}, bf16[64,32,128]{2,1,0:T(8,128)(2,1)}, u32[]{:S(2)}) copy-start(bf16[64,32,128]{2,1,0:T(8,128)(2,1)} %param.9) | copy-start | bytes 1572868
  47.3 380.5 %all-to-all-start.1 = ((bf16[128,12,32,128]{3,2,1,0:T(8,128)(2,1)}), bf16[128,12,32,128]{3,2,1,0:T(8,128)(2,1)}, u32[]{:S(2)}, u32[]{:S(2)}) async-start(bf16[128,12,32,128]{3,2,1,0:T(8,128)(2,1)} %broadcast_select_fusion.1), calls=%async_computation.1 | async-start | bytes 25165824 | tf_op jit(solution)/shard_map/all_to_all | solution.py:39
  61.6 523.6 %all-reduce.2.cloned.1.call-start = ((), (), s32[]{:S(2)}) async-start(), calls=%async_computation.3 | async-start | bytes 1572864 | tf_op jit(solution)/shard_map/pmax | solution.py:48
  427.8 186.3 %copy-start.3 = (s32[128]{0:T(128)S(1)}, s32[128]{0:T(128)}, u32[]{:S(2)}) copy-start(s32[128]{0:T(128)} %param.13) | copy-start | bytes 1540
Sparse Core Ops, SparseCore 0:
  487.2 97.9 all-reduce.1
where the time goes:
time: 623 us; the launch traced here: 622 us
  waiting for transfers between devices  464 us (74%)
  local copies, waits for them, and re-layouts  42.4 us (7%)
  starting transfers between devices  32.7 us (5%)
  blocking collectives  27.4 us (4%)
  matrix products  25.9 us (4%)
  other arithmetic  15.4 us (2%)
  between operations  13.5 us (2%)
    all_to_all x1, waiting for transfers between devices, local(): lax.all_to_all(rows, 'shard', split_axis=0, concat_axis=0, tiled=True)  366 us
    pmax x1, waiting for transfers between devices, local(): maxima = lax.pmax(maxima, 'blk')  98.1 us
    all_to_all x1, blocking collectives, local(): lax.all_to_all(totals, 'shard', split_axis=0, concat_axis=0, tiled=True)  27.4 us
    dot_general x12, matrix products, block_maxima(): jnp.einsum('oer,ogr->oeg', query_tile_rows, token_vectors, preferred_elem...  25.9 us
    all_to_all x1, starting transfers between devices, local(): lax.all_to_all(jnp.stack([global_query, pair_passage], axis=2), 'shard',...  18.4 us
    gather x12, local copies, waits for them, and re-layouts, block_maxima(): live = positions[None, :] < jnp.take(lengths, passage_idx)[:, None]  14.7 us
    all_to_all x1, starting transfers between devices, local(): lax.all_to_all(rows, 'shard', split_axis=0, concat_axis=0, tiled=True)  14.3 us
  transfers between devices with their start and end apart: 3, of which 2 were waited for; matrix products, arithmetic and copies ran while one was open for 3% of the time, Pallas kernels for 0%

commit v1 on v0

v1 whole, which is shorter than its diff:
```python
import functools
import math

import jax
import jax.numpy as jnp
from jax import lax
from jax.experimental import pallas as pl
from jax.experimental.pallas import tpu as pltpu
from jax.sharding import PartitionSpec as P

NT = (((1,), (1,)), ((), ()))

def kernel(side, xs, q_dev, q_ref, p_ref, len_ref, pq_ref, pp_ref, cnt_ref, o_ref,
           qs, ps, w, wx, rows, table, idx, outs,
           qa_send, qa_recv, ring_send, ring_recv, sib_send, sib_recv,
           px_send, px_recv, px_local, wx_send, wx_recv, row_send, row_recv, out_send, out_recv):
    me = lax.axis_index("shard")
    x = lax.axis_index("blk")
    core = me % 2
    zz = (me // 2) % side
    yy = me // (2 * side)
    f = zz + core * (yy - zz)
    g = yy + core * (zz - yy)

    def owner(c, ff, gg):
        return c + ff * (2 + c * (2 * side - 2)) + gg * (2 * side - c * (2 * side - 2))

    def wrap(value, size):
        return (value + 2 * size) % size

    sibling = {"shard": me + 1 - 2 * core}

    def first(o):
        return {"shard": owner(core, wrap(f + o, side), g)}

    def second(o):
        return {"shard": owner(core, f, wrap(g + o, side))}

    def along_x(o):
        return {"blk": wrap(x + o, xs)}

    barrier = pltpu.get_barrier_semaphore()
    near = sorted({1 % side, (side - 1) % side})
    friends = ([first(o) for o in range(1, side)] + [second(o) for o in near] + [sibling]
               + [along_x(o) for o in range(1, xs)])
    for friend in friends:
        pl.semaphore_signal(barrier, inc=1, device_id=friend, device_id_type=pl.DeviceIdType.MESH)
    pl.semaphore_wait(barrier, len(friends))

    def remote(src, dst, send, recv, to):
        return pltpu.make_async_remote_copy(src_ref=src, dst_ref=dst, send_sem=send, recv_sem=recv,
                                            device_id=to, device_id_type=pl.DeviceIdType.MESH)

    held = ps.shape[0]
    q_rows = q_ref.shape[0]

    qa = [remote(q_ref, qs.at[core, g, f], qa_send.at[o], qa_recv.at[o], first(o)) for o in range(1, side)]
    for copy in qa:
        copy.start()
    px = [remote(p_ref.at[pl.ds(wrap(x + o, xs) * held, held)], ps.at[:, x], px_send.at[o], px_recv.at[o],
                 along_x(o)) for o in range(1, xs)]
    for copy in px:
        copy.start()
    px_own = pltpu.make_async_copy(p_ref.at[pl.ds(x * held, held)], ps.at[:, x], px_local)
    px_own.start()
    qs[core, g, f] = q_ref[...]

    slots = pq_ref.shape[0]
    wanted = pq_ref[...] * (held * xs) + pp_ref[...]
    owners = wanted.shape[1]
    wanted = jnp.concatenate([wanted, jnp.zeros((128 - slots, owners), jnp.int32)], axis=0)
    idx[...] = wanted.T

    n = side * q_rows

    tokens = q_rows // q_dev
    lane = lax.broadcasted_iota(jnp.int32, (q_dev * side, n), 1)
    line = lax.broadcasted_iota(jnp.int32, (q_dev * side, n), 0)
    member = jnp.where((line % side) * q_dev + line // side == lane // tokens, 1.0, 0.0).astype(jnp.bfloat16)

    plen = ps.shape[1] * ps.shape[2]
    dim = ps.shape[3]

    def score(c, gg):
        queries = qs[c, gg].reshape(n, dim)
        sims = lax.dot_general(ps[...].reshape(held * plen, dim), queries, NT, preferred_element_type=jnp.float32)
        best = jnp.max(sims.reshape(held, plen, n), axis=1)
        high = best.astype(jnp.bfloat16)
        rest = best - high.astype(jnp.float32)
        mid = rest.astype(jnp.bfloat16)
        low = (rest - mid.astype(jnp.float32)).astype(jnp.bfloat16)
        total = (lax.dot_general(member, high, NT, preferred_element_type=jnp.float32)
                 + lax.dot_general(member, mid, NT, preferred_element_type=jnp.float32)
                 + lax.dot_general(member, low, NT, preferred_element_type=jnp.float32))
        blank = jnp.zeros((side, 128 - held), jnp.float32)
        line_w = jnp.zeros((side, 128), jnp.float32)
        for q in range(q_dev):
            part = jnp.concatenate([total[q * side:(q + 1) * side], blank], axis=1)
            line_w = line_w + pltpu.roll(part, q * held * xs + x * held, 1)
        w[c, gg] = line_w

    def place(m):
        return wrap(g - (2 * (m % 2) - 1) * ((m + 1) // 2), side)

    def sib_place(m):
        return wrap(f - (2 * (m % 2) - 1) * ((m + 1) // 2), side)

    def pass_on(m, at, way):
        slab = qs.at[core, at]
        return remote(slab, slab, ring_send, ring_recv.at[m + 2], second(way))

    def to_sibling(m, at):
        slab = qs.at[core, at]
        return remote(slab, slab, sib_send, sib_recv.at[m], sibling)

    for copy in qa:
        copy.wait_recv()
    remote(qs.at[core, g], qs.at[core, g], ring_send, ring_recv.at[1], second(1)).start()
    if side > 2:
        remote(qs.at[core, g], qs.at[core, g], ring_send, ring_recv.at[2], second(-1)).start()
    to_sibling(0, g).start()

    px_own.wait()
    for copy in px:
        copy.wait_recv()
    def pad(i, _):
        token = lax.broadcasted_iota(jnp.int32, (plen, dim), 0)
        vectors = ps[i].reshape(plen, dim).astype(jnp.float32)
        kept = jnp.where(token < len_ref[x * held + i], vectors, vectors[0:1, :])
        ps[i] = kept.astype(jnp.bfloat16).reshape(ps.shape[1:])
        return 0
    lax.fori_loop(0, held, pad, 0)

    score(core, g)

    def step(m, _):
        at = place(m)
        slab = qs.at[core, at]
        remote(slab, slab, ring_send, ring_recv.at[m], sibling).wait_recv()

        @pl.when(m <= side - 3)
        def _():
            pass_on(m, at, 2 * (m % 2) - 1).start()

        to_sibling(m, at).start()
        other = sib_place(m - 1)
        slab = qs.at[1 - core, other]
        remote(slab, slab, sib_send, sib_recv.at[m - 1], sibling).wait_recv()
        score(core, at)
        score(1 - core, other)
        return 0
    lax.fori_loop(1, side, step, 0)
    last = sib_place(side - 1)
    slab = qs.at[1 - core, last]
    remote(slab, slab, sib_send, sib_recv.at[side - 1], sibling).wait_recv()
    score(1 - core, last)

    share = side // xs
    wxs = [remote(w.at[:, pl.ds(wrap(x + o, xs) * share, share)], wx.at[o], wx_send.at[o], wx_recv.at[o], along_x(o))
           for o in range(1, xs)]
    for copy in wxs:
        copy.start()
    full = w[:, pl.ds(x * share, share)]
    for o, copy in zip(range(1, xs), wxs):
        copy.wait_recv()
        full = full + wx[o]
    targets = 2 * share * side
    rows[...] = full.reshape(targets, 1, 128)

    def row(k, _):
        k = (k + me) % targets
        to = owner(k // (share * side), k % side, x * share + (k // side) % share)

        @pl.when(to != me)
        def _():
            remote(rows.at[k], table.at[me], row_send, row_recv, {"shard": to}).start()

        @pl.when(to == me)
        def _():
            table[me] = rows[k]
        return 0
    lax.fori_loop(0, targets, row, 0)

    home = g // share
    out_copies = [remote(outs, outs, out_send.at[o], out_recv, along_x(o)) for o in range(1, xs)]

    @pl.when(home == x)
    def _():
        lead = table.at[pl.ds(0, owners - 1)]
        remote(lead, lead, row_send, row_recv, sibling).wait_recv()
        picked = jnp.take_along_axis(table[...].reshape(owners, 128), idx[...], axis=1, mode="promise_in_bounds")
        picked = picked.T[:slots, :]
        slot = lax.broadcasted_iota(jnp.int32, (slots, owners), 0)
        outs[...] = jnp.where(slot < cnt_ref[...], picked, 0.0)
        for copy in out_copies:
            copy.start()
        o_ref[...] = outs[...]
        for copy in out_copies:
            copy.wait_send()
        lead = rows.at[pl.ds(0, targets - 1)]
        remote(lead, lead, row_send, row_recv, sibling).wait_send()

    @pl.when(home != x)
    def _():
        out_copies[0].wait_recv()
        o_ref[...] = outs[...]
        remote(rows, rows, row_send, row_recv, sibling).wait_send()

    for copy in qa:
        copy.wait_send()
    for copy in px:
        copy.wait_send()
    for copy in wxs:
        copy.wait_send()
    lead = qs.at[core, pl.ds(0, side - 1)]
    remote(lead, lead, ring_send, ring_recv.at[0], sibling).wait_send()
    remote(qs.at[core], qs.at[core], sib_send, sib_recv.at[0], sibling).wait_send()

def local(side, xs, queries, passages, lengths, pair_query, pair_passage, send_counts):
    owners, slots = pair_query.shape
    q_dev, q_tokens, dim = queries.shape
    per_owner, block, _ = passages.shape
    held = per_owner // xs
    share = side // xs
    vmem = pl.BlockSpec(memory_space=pltpu.VMEM)
    dma = pltpu.SemaphoreType.DMA
    out = pl.pallas_call(
        functools.partial(kernel, side, xs, q_dev),
        out_shape=jax.ShapeDtypeStruct((slots, owners), jnp.float32),
        in_specs=[vmem, pl.BlockSpec(memory_space=pl.ANY), pl.BlockSpec(memory_space=pltpu.SMEM), vmem, vmem, vmem],
        out_specs=vmem,
        scratch_shapes=[
            pltpu.VMEM((2, side, side, q_dev * q_tokens, dim), jnp.bfloat16),
            pltpu.VMEM((held, xs, block, dim), jnp.bfloat16),
            pltpu.VMEM((2, side, side, 128), jnp.float32),
            pltpu.VMEM((xs, 2, share, side, 128), jnp.float32),
            pltpu.VMEM((2 * share * side, 1, 128), jnp.float32),
            pltpu.VMEM((owners, 1, 128), jnp.float32),
            pltpu.VMEM((owners, 128), jnp.int32),
            pltpu.VMEM((slots, owners), jnp.float32),
            dma((side,)), dma((side,)), dma, dma((side + 2,)), dma, dma((side,)),
            dma((xs,)), dma((xs,)), dma, dma((xs,)), dma((xs,)), dma, dma, dma((xs,)), dma,
        ],
        compiler_params=pltpu.CompilerParams(
            collective_id=0, has_side_effects=True, vmem_limit_bytes=48 * 2**20),
        cost_estimate=pl.CostEstimate(
            flops=2 * per_owner * block * owners * q_dev * q_tokens * dim, bytes_accessed=8 * 2**20,
            transcendentals=0),
    )(queries.reshape(q_dev * q_tokens, dim), passages, lengths,
      pair_query.T, pair_passage.T, send_counts.reshape(1, owners))
    return out.T

def solution(mesh):
    placed = (
        P("shard", None, None),
        P("shard", "blk", None),
        P("shard"),
        P("shard", None),
        P("shard", None),
        P("shard"),
    )
    side = math.isqrt(mesh.shape["shard"] // 2)
    return jax.shard_map(
        functools.partial(local, side, mesh.shape["blk"]),
        mesh=mesh, in_specs=placed, out_specs=P("shard", None), check_vma=False
    )
```

time: 623 us -> 58.5 us (0.09)
  the two profiles are of different devices: /device:TPU:1 before, /device:TPU:4 now
where the time goes in v1:
time: 58.5 us; the launch traced here: 58.1 us
  Pallas kernels  53.7 us (92%)
  local copies, waits for them, and re-layouts  4.42 us (8%)
    pallas_call x1, Pallas kernels, local(): pl.pallas_call(functools.partial(kernel, side, xs, q_dev), out_shape=jax....  53.7 us
    unnamed x13, local copies, waits for them, and re-layouts  4.42 us

profile of v1, /device:TPU:4, one launch (start us, length us, event | category | flops | bytes accessed | tf_op | source)
XLA Modules:
  0.0 58.1 jit_solution(740643625498683071)
XLA Ops:
  0.0 0.0 copy-start.4
  0.0 0.0 copy-start.5
  0.0 0.7 %copy-done.4 = s32[64]{0:T(128)S(1)} copy-done((s32[64]{0:T(128)S(1)}, s32[64]{0:T(128)}, u32[]{:S(2)}) %copy-start.4) | copy-done | bytes 280
  0.7 0.0 copy-done.5
  0.7 0.0 copy-start
  0.7 1.0 %copy-done = bf16[64,32,128]{2,1,0:T(8,128)(2,1)S(1)} copy-done((bf16[64,32,128]{2,1,0:T(8,128)(2,1)S(1)}, bf16[64,32,128]{2,1,0:T(8,128)(2,1)}, u32[]{:S(2)}) %copy-start) | copy-done | bytes 524312
  1.7 0.0 copy-start.1
  1.7 0.7 %copy-done.1 = bf16[2,32,128]{2,1,0:T(8,128)(2,1)S(1)} copy-done((bf16[2,32,128]{2,1,0:T(8,128)(2,1)S(1)}, bf16[2,32,128]{2,1,0:T(8,128)(2,1)}, u32[]{:S(2)}) %copy-start.1) | copy-done | bytes 16408
  2.4 0.0 copy-start.2
  2.4 0.7 %copy-done.2 = s32[128,12]{0,1:T(8,128)S(1)} copy-done((s32[128,12]{0,1:T(8,128)S(1)}, s32[128,12]{0,1:T(8,128)}, u32[]{:S(2)}) %copy-start.2) | copy-done | bytes 6168
  3.1 0.0 copy-start.3
  3.1 0.7 %copy-done.3 = s32[128,12]{0,1:T(8,128)S(1)} copy-done((s32[128,12]{0,1:T(8,128)S(1)}, s32[128,12]{0,1:T(8,128)}, u32[]{:S(2)}) %copy-start.3) | copy-done | bytes 6168
  3.8 53.7 %shard_map.64 = f32[12,128]{1,0:T(8,128)S(1)} custom-call(bf16[64,128]{1,0:T(8,128)(2,1)S(1)} %bitcast.6, bf16[64,32,128]{2,1,0:T(8,128)(2,1)S(1)} %copy-done, s32[64]{0:T(128)S(1)} %copy-done.4, s32[12,128]{1,0:T(8,128)S(1)} %bitcast.7, s32[12,128]{1,0:T(8,128)S(1)} %bitcast.8, s32[1,128]{1,0:T(1,128)S(1)} %bitcast.9), custom_call_target="tpu_custom_call" | custom-call | flops 4294967296 | bytes 8388608 | tf_op jit(solution)/shard_map/pallas_call | solution.py:227
  57.5 0.6 %copy.8 = f32[128,12]{0,1:T(8,128)} copy(f32[128,12]{0,1:T(8,128)S(1)} %bitcast.5) | data formatting | bytes 12288
Async XLA Ops:
  0.0 0.7 %copy-start.4 = (s32[64]{0:T(128)S(1)}, s32[64]{0:T(128)}, u32[]{:S(2)}) copy-start(s32[64]{0:T(128)} %len_ref.1) | copy-start | bytes 772
  0.0 0.7 %copy-start.5 = (s32[128]{0:T(128)S(1)}, s32[128]{0:T(128)}, u32[]{:S(2)}) copy-start(s32[128]{0:T(128)} %param.11) | copy-start | bytes 1540
  0.7 1.0 %copy-start = (bf16[64,32,128]{2,1,0:T(8,128)(2,1)S(1)}, bf16[64,32,128]{2,1,0:T(8,128)(2,1)}, u32[]{:S(2)}) copy-start(bf16[64,32,128]{2,1,0:T(8,128)(2,1)} %p_ref.1) | copy-start | bytes 1572868
  1.7 0.7 %copy-start.1 = (bf16[2,32,128]{2,1,0:T(8,128)(2,1)S(1)}, bf16[2,32,128]{2,1,0:T(8,128)(2,1)}, u32[]{:S(2)}) copy-start(bf16[2,32,128]{2,1,0:T(8,128)(2,1)} %param.6) | copy-start | bytes 49156
  2.4 0.7 %copy-start.2 = (s32[128,12]{0,1:T(8,128)S(1)}, s32[128,12]{0,1:T(8,128)}, u32[]{:S(2)}) copy-start(s32[128,12]{0,1:T(8,128)} %param.9) | copy-start | bytes 18436
  3.1 0.7 %copy-start.3 = (s32[128,12]{0,1:T(8,128)S(1)}, s32[128,12]{0,1:T(8,128)}, u32[]{:S(2)}) copy-start(s32[128,12]{0,1:T(8,128)} %param.10) | copy-start | bytes 18436

commit v2 on v0

v2 whole, which is shorter than its diff:
```python
import functools
import math

import jax
import jax.numpy as jnp
from jax import lax
from jax.experimental import pallas as pl
from jax.experimental.pallas import tpu as pltpu
from jax.sharding import PartitionSpec as P

NT = (((1,), (1,)), ((), ()))
ORDER = (0, 4, 1, 2, -2, 3, -3, -1)


def kernel(side, xs, q_dev, q_hbm, p_hbm, len_hbm, pq_hbm, pp_hbm, cnt_hbm, o_ref,
           len_ref, pq_ref, pp_ref, cnt_ref, qs, ps, rows, table, idx, outs,
           in_sems, near_send, near_recv, far_recv, opp_send, opp_recv, ring_send, ring_recv, sib_send, sib_recv,
           px_send, px_recv, px_local, row_send, row_recv, out_send, out_recv):
    me = lax.axis_index("shard")
    x = lax.axis_index("blk")
    core = me % 2
    zz = (me // 2) % side
    yy = me // (2 * side)
    f = zz + core * (yy - zz)
    g = yy + core * (zz - yy)
    half = side // 2

    def wrap(value, size):
        return (value + 2 * size) % size

    def at(ff, gg):
        ff, gg = wrap(ff, side), wrap(gg, side)
        return {"shard": core + ff * (2 + core * (2 * side - 2)) + gg * (2 * side - core * (2 * side - 2))}

    def along_x(o):
        return {"blk": wrap(x + o, xs)}

    sibling = {"shard": me + 1 - 2 * core}

    def remote(src, dst, send, recv, to):
        return pltpu.make_async_remote_copy(src_ref=src, dst_ref=dst, send_sem=send, recv_sem=recv,
                                            device_id=to, device_id_type=pl.DeviceIdType.MESH)

    sources = [(len_hbm, len_ref), (pq_hbm, pq_ref), (pp_hbm, pp_ref), (cnt_hbm, cnt_ref), (q_hbm, qs.at[g, f])]
    small = [pltpu.make_async_copy(src, dst, in_sems.at[i]) for i, (src, dst) in enumerate(sources)]
    for copy in small:
        copy.start()

    barrier = pltpu.get_barrier_semaphore()
    friends = ([at(f + o, g) for o in range(1, side)] + [at(f, g + o) for o in (1, -1, 2, -2, half)] + [sibling]
               + [along_x(o) for o in range(1, xs)])
    for friend in friends:
        pl.semaphore_signal(barrier, inc=1, device_id=friend, device_id_type=pl.DeviceIdType.MESH)
    pl.semaphore_wait(barrier, len(friends))

    held = ps.shape[1]
    q_rows = q_hbm.shape[0]

    remote(q_hbm, qs.at[g, f], near_send, far_recv, at(f, g + half)).start()
    for o in range(1, side):
        remote(q_hbm, qs.at[g, f], near_send, near_recv, at(f + o, g)).start()
    px = [remote(p_hbm.at[pl.ds(wrap(x + o, xs) * held, held)], ps.at[core, :, x], px_send.at[o], px_recv.at[o],
                 along_x(o)) for o in range(1, xs)]
    for copy in px:
        copy.start()
    px_own = pltpu.make_async_copy(p_hbm.at[pl.ds(x * held, held)], ps.at[core, :, x], px_local)
    px_own.start()

    for copy in small:
        copy.wait()
    slots = pq_ref.shape[0]
    wanted = pq_ref[...] * (held * xs) + pp_ref[...]
    owners = wanted.shape[1]
    wanted = jnp.concatenate([wanted, jnp.zeros((128 - slots, owners), jnp.int32)], axis=0)
    idx[...] = wanted.T

    n = side * q_rows
    tokens = q_rows // q_dev
    lane = lax.broadcasted_iota(jnp.int32, (q_dev * side, n), 1)
    line = lax.broadcasted_iota(jnp.int32, (q_dev * side, n), 0)
    member = jnp.where((line % side) * q_dev + line // side == lane // tokens, 1.0, 0.0).astype(jnp.bfloat16)

    plen = ps.shape[2] * ps.shape[3]
    dim = ps.shape[4]

    def score(gg, c):
        queries = qs[gg].reshape(n, dim)
        sims = lax.dot_general(ps[c].reshape(held * plen, dim), queries, NT, preferred_element_type=jnp.float32)
        best = jnp.max(sims.reshape(held, plen, n), axis=1)
        high = best.astype(jnp.bfloat16)
        rest = best - high.astype(jnp.float32)
        mid = rest.astype(jnp.bfloat16)
        low = (rest - mid.astype(jnp.float32)).astype(jnp.bfloat16)
        total = (lax.dot_general(member, high, NT, preferred_element_type=jnp.float32)
                 + lax.dot_general(member, mid, NT, preferred_element_type=jnp.float32)
                 + lax.dot_general(member, low, NT, preferred_element_type=jnp.float32))
        blank = jnp.zeros((side, 128 - held), jnp.float32)
        line_w = jnp.zeros((side, 128), jnp.float32)
        for q in range(q_dev):
            part = jnp.concatenate([total[q * side:(q + 1) * side], blank], axis=1)
            line_w = line_w + pltpu.roll(part, q * held * xs + x * held, 1)
        rows[c, gg] = line_w.reshape(side, 1, 128)

    def send_rows(gg, start):
        for o in range(start, side):
            ff = wrap(f + o, side)
            remote(rows.at[:, gg, ff], table.at[pl.ds(2 * (me // 2), 2)], row_send, row_recv, at(ff, gg)).start()

    def arrived(gg, d):
        remote(qs.at[gg], qs.at[gg], ring_send, ring_recv.at[d], sibling).wait_recv()

    def pass_on(gg, o):
        remote(qs.at[gg], qs.at[gg], ring_send, ring_recv.at[wrap(gg - g - o, side)], at(f, g + o)).start()

    opposite = wrap(g + half, side)
    remote(q_hbm, qs.at[opposite, f], near_send, far_recv, sibling).wait_recv()
    for o in range(1, side):
        remote(qs.at[opposite, f], qs.at[opposite, f], opp_send, opp_recv, at(f + o, g)).start()
    seven = qs.at[g, pl.ds(0, side - 1)]
    remote(seven, seven, near_send, near_recv, sibling).wait_recv()
    for o in (1, -1, 2, -2):
        pass_on(g, o)

    px_own.wait()
    for copy in px:
        copy.wait_recv()

    def pad(i, _):
        token = lax.broadcasted_iota(jnp.int32, (plen, dim), 0)
        vectors = ps[core, i].reshape(plen, dim).astype(jnp.float32)
        kept = jnp.where(token < len_ref[x * held + i], vectors, vectors[0:1, :])
        ps[core, i] = kept.astype(jnp.bfloat16).reshape(ps.shape[2:])
        return 0
    lax.fori_loop(0, held, pad, 0)
    share = remote(ps.at[core], ps.at[core], sib_send, sib_recv, sibling)
    share.start()

    score(g, core)
    remote(seven, seven, opp_send, opp_recv, sibling).wait_recv()
    for o in (1, -1):
        pass_on(opposite, o)
    share.wait_recv()
    score(g, 1 - core)
    send_rows(g, 1)
    table[pl.ds(2 * (me // 2), 2)] = rows[:, g, f]

    def step(k, _):
        d = sum(jnp.where(k == i, o, 0) for i, o in enumerate(ORDER))
        gg = wrap(g + d, side)

        @pl.when(k > 1)
        def _():
            arrived(gg, wrap(d, side))
        score(gg, core)
        score(gg, 1 - core)
        send_rows(gg, 0)
        return 0
    lax.fori_loop(1, side, step, 0)

    rest = table.at[pl.ds(0, owners - 2)]
    remote(rest, rest, row_send, row_recv, sibling).wait_recv()
    picked = jnp.take_along_axis(table[...].reshape(owners, 128), idx[...], axis=1, mode="promise_in_bounds")
    picked = picked.T[:slots, :]
    slot = lax.broadcasted_iota(jnp.int32, (slots, owners), 0)
    outs[0] = jnp.where(slot < cnt_ref[...], picked, 0.0)
    out_copies = [remote(outs.at[0], outs.at[o], out_send.at[o], out_recv.at[o], along_x(o)) for o in range(1, xs)]
    for copy in out_copies:
        copy.start()
    total = outs[0]
    for o, copy in zip(range(1, xs), out_copies):
        copy.wait_recv()
        total = total + outs[o]
    o_ref[...] = total

    for copy in out_copies + px + [share]:
        copy.wait_send()
    remote(qs.at[g], qs.at[g], near_send, far_recv, sibling).wait_send()
    remote(seven, seven, opp_send, opp_recv, sibling).wait_send()
    six = qs.at[pl.ds(0, 6)]
    remote(six, six, ring_send, ring_recv.at[0], sibling).wait_send()
    remote(rest, rest, row_send, row_recv, sibling).wait_send()


def local(side, xs, queries, passages, lengths, pair_query, pair_passage, send_counts):
    owners, slots = pair_query.shape
    q_dev, q_tokens, dim = queries.shape
    per_owner, block, _ = passages.shape
    held = per_owner // xs
    dma = pltpu.SemaphoreType.DMA
    out = pl.pallas_call(
        functools.partial(kernel, side, xs, q_dev),
        out_shape=jax.ShapeDtypeStruct((slots, owners), jnp.float32),
        in_specs=[pl.BlockSpec(memory_space=pltpu.HBM)] * 6,
        out_specs=pl.BlockSpec(memory_space=pltpu.VMEM),
        scratch_shapes=[
            pltpu.SMEM((per_owner,), jnp.int32),
            pltpu.VMEM((slots, owners), jnp.int32),
            pltpu.VMEM((slots, owners), jnp.int32),
            pltpu.VMEM((1, owners), jnp.int32),
            pltpu.VMEM((side, side, q_dev * q_tokens, dim), jnp.bfloat16),
            pltpu.VMEM((2, held, xs, block, dim), jnp.bfloat16),
            pltpu.VMEM((2, side, side, 1, 128), jnp.float32),
            pltpu.VMEM((owners, 1, 128), jnp.float32),
            pltpu.VMEM((owners, 128), jnp.int32),
            pltpu.VMEM((xs, slots, owners), jnp.float32),
            dma((5,)), dma, dma, dma, dma, dma, dma, dma((side,)), dma, dma,
            dma((xs,)), dma((xs,)), dma, dma, dma, dma((xs,)), dma((xs,)),
        ],
        compiler_params=pltpu.CompilerParams(
            collective_id=0, has_side_effects=True, vmem_limit_bytes=60 * 2**20),
        cost_estimate=pl.CostEstimate(
            flops=2 * per_owner * block * owners * q_dev * q_tokens * dim, bytes_accessed=8 * 2**20,
            transcendentals=0),
    )(queries.reshape(q_dev * q_tokens, dim), passages, lengths,
      pair_query.T, pair_passage.T, send_counts.reshape(1, owners))
    return out.T


def solution(mesh):
    placed = (
        P("shard", None, None),
        P("shard", "blk", None),
        P("shard"),
        P("shard", None),
        P("shard", None),
        P("shard"),
    )
    side = math.isqrt(mesh.shape["shard"] // 2)
    return jax.shard_map(
        functools.partial(local, side, mesh.shape["blk"]),
        mesh=mesh, in_specs=placed, out_specs=P("shard", None), check_vma=False
    )
```

time: 623 us -> 49.7 us (0.08)
  the two profiles are of different devices: /device:TPU:1 before, /device:TPU:56 now
where the time goes in v2:
time: 49.7 us; the launch traced here: 49.6 us
  Pallas kernels  48.3 us (97%)
  local copies, waits for them, and re-layouts  1.3 us (3%)
    pallas_call x1, Pallas kernels, local(): pl.pallas_call(functools.partial(kernel, side, xs, q_dev), out_shape=jax....  48.3 us
    unnamed x1, local copies, waits for them, and re-layouts  1.3 us

profile of v2, /device:TPU:56, one launch (start us, length us, event | category | flops | bytes accessed | tf_op | source)
XLA Modules:
  0.0 49.6 jit_solution(447264943787854725)
XLA Ops:
  0.0 48.3 %shard_map.64 = f32[12,128]{1,0:T(8,128)} custom-call(bf16[64,128]{1,0:T(8,128)(2,1)} %bitcast.6, bf16[64,32,128]{2,1,0:T(8,128)(2,1)} %p_hbm.1, s32[64]{0:T(128)} %len_hbm.1, s32[12,128]{1,0:T(8,128)} %bitcast.7, s32[12,128]{1,0:T(8,128)} %bitcast.8, s32[1,128]{1,0:T(1,128)} %bitcast.9), custom_call_target="tpu_custom_call" | custom-call | flops 4294967296 | bytes 8388608 | tf_op jit(solution)/shard_map/pallas_call | solution.py:190
  48.3 1.3 %copy.8 = f32[128,12]{0,1:T(8,128)} copy(f32[128,12]{0,1:T(8,128)} %bitcast.5) | data formatting | bytes 12288

commit v3 on v2

v3 whole, which is shorter than its diff:
```python
import functools
import math

import jax
import jax.numpy as jnp
from jax import lax
from jax.experimental import pallas as pl
from jax.experimental.pallas import tpu as pltpu
from jax.sharding import PartitionSpec as P

NT = (((1,), (1,)), ((), ()))


def kernel(side, xs, q_dev, q_hbm, p_hbm, len_hbm, pq_hbm, pp_hbm, cnt_hbm, o_ref,
           len_ref, len_far, pq_ref, pp_ref, cnt_ref, qs, raw, ps, maxima, rows, table, idx, outs,
           in_sems, len_send, len_recv, near_send, near_recv, line_send, line_recv, sib_send, sib_recv,
           px_send, px_recv, px_local, row_send, row_recv, out_send, out_recv):
    me = lax.axis_index("shard")
    x = lax.axis_index("blk")
    core = me % 2
    zz = (me // 2) % side
    yy = me // (2 * side)
    f = zz + core * (yy - zz)
    g = yy + core * (zz - yy)

    def wrap(value, size):
        return (value + 2 * size) % size

    def at(ff, gg):
        ff, gg = wrap(ff, side), wrap(gg, side)
        return {"shard": core + ff * (2 + core * (2 * side - 2)) + gg * (2 * side - core * (2 * side - 2))}

    def along_x(o):
        return {"blk": wrap(x + o, xs)}

    sibling = {"shard": me + 1 - 2 * core}

    def remote(src, dst, send, recv, to):
        return pltpu.make_async_remote_copy(src_ref=src, dst_ref=dst, send_sem=send, recv_sem=recv,
                                            device_id=to, device_id_type=pl.DeviceIdType.MESH)

    barrier = pltpu.get_barrier_semaphore()
    friends = ([along_x(o) for o in (2, 1, 3)] + [at(f + o, g) for o in (4, 3, 5, 2, 6, 1, 7)]
               + [at(f, g + o) for o in (4, 3, 5, 2, 6, 1, 7)] + [sibling])
    for friend in friends:
        pl.semaphore_signal(barrier, inc=1, device_id=friend, device_id_type=pl.DeviceIdType.MESH)
    sources = [(len_hbm, len_ref), (pq_hbm, pq_ref), (pp_hbm, pp_ref), (cnt_hbm, cnt_ref), (q_hbm, qs.at[zz, yy])]
    small = [pltpu.make_async_copy(src, dst, in_sems.at[i]) for i, (src, dst) in enumerate(sources)]
    for copy in small:
        copy.start()

    pl.semaphore_wait(barrier, len(friends))

    held = ps.shape[1]
    q_rows = q_hbm.shape[0]

    px = [remote(p_hbm.at[pl.ds(wrap(x + o, xs) * held, held)], raw.at[core, x], px_send.at[o], px_recv.at[o],
                 along_x(o)) for o in range(1, xs)]
    for o in (2, 1, 3):
        px[o - 1].start()
    for o in range(1, side):
        remote(q_hbm, qs.at[zz, yy], near_send, near_recv.at[f], at(f + o, g)).start()
    own = p_hbm.at[pl.ds(x * held, held)]
    px_own = pltpu.make_async_copy(own, raw.at[core, x], px_local)
    px_own.start()

    def block(o):
        return raw.at[core, wrap(x - o, xs)]

    share = [remote(own, block(0), sib_send.at[0], sib_recv.at[0], sibling)]
    share += [remote(block(o), block(o), sib_send.at[o], sib_recv.at[o], sibling) for o in range(1, xs)]
    share[0].start()
    lens_out = remote(len_hbm, len_far, len_send, len_recv, sibling)
    lens_out.start()

    for copy in small:
        copy.wait()
    slots = pq_ref.shape[0]
    wanted = pq_ref[...] * (held * xs) + pp_ref[...]
    owners = wanted.shape[1]
    wanted = jnp.concatenate([wanted, jnp.zeros((128 - slots, owners), jnp.int32)], axis=0)
    idx[...] = wanted.T

    n = side * q_rows
    tokens = q_rows // q_dev
    lane = lax.broadcasted_iota(jnp.int32, (q_dev * side, n), 1)
    line = lax.broadcasted_iota(jnp.int32, (q_dev * side, n), 0)
    member = jnp.where((line % side) * q_dev + line // side == lane // tokens, 1.0, 0.0).astype(jnp.bfloat16)

    plen = ps.shape[2] * ps.shape[3]
    dim = ps.shape[4]

    def best_match(gg):
        sims = lax.dot_general(ps[...].reshape(2 * held * plen, dim), qs[gg].reshape(n, dim), NT,
                               preferred_element_type=jnp.float32)
        return jnp.max(sims.reshape(2 * held, plen, n), axis=1)

    def add_up(best, gg):
        high = best.astype(jnp.bfloat16)
        rest = best - high.astype(jnp.float32)
        mid = rest.astype(jnp.bfloat16)
        low = (rest - mid.astype(jnp.float32)).astype(jnp.bfloat16)
        total = (lax.dot_general(member, high, NT, preferred_element_type=jnp.float32)
                 + lax.dot_general(member, mid, NT, preferred_element_type=jnp.float32)
                 + lax.dot_general(member, low, NT, preferred_element_type=jnp.float32))
        blank = jnp.zeros((side, 128 - held), jnp.float32)
        for c in range(2):
            line_w = jnp.zeros((side, 128), jnp.float32)
            for q in range(q_dev):
                part = total[q * side:(q + 1) * side, c * held:(c + 1) * held]
                part = jnp.concatenate([part, blank], axis=1)
                line_w = line_w + pltpu.roll(part, q * held * xs + x * held, 1)
            rows[c, gg] = line_w.reshape(side, 1, 128)

    mine = table.at[pl.ds(2 * (me // 2), 2)]

    def owner_at(y, z):
        return {"shard": (y * side + z) * 2 + core}

    def send_rows(z):
        for o in range(1, side):
            y = wrap(yy + o, side)
            remote(rows.at[:, z, y], mine, row_send, row_recv, owner_at(y, z)).start()

        @pl.when(z != zz)
        def _():
            remote(rows.at[:, z, yy], mine, row_send, row_recv, owner_at(yy, z)).start()

    def near_arrived(ff):
        block = qs.at[zz, yy]
        remote(block, block, near_send, near_recv.at[ff], sibling).wait_recv()

    @pl.when(core == 1)
    def _():
        for o in range(1, side):
            near_arrived(wrap(f + o, side))
        for o in (1, -1, 2, -2):
            remote(qs.at[zz], qs.at[zz], line_send, line_recv.at[zz], at(f, g + o)).start()

    @pl.when(core == 0)
    def _():
        for z in range(0, side, 2):
            for ff in (z, z + 1):
                @pl.when(ff != f)
                def _():
                    near_arrived(ff)
            pair = qs.at[pl.ds(z, 2), yy]
            for o in (4, 3, 5, 2, 6, 1, 7):
                remote(pair, pair, line_send, line_recv.at[z], at(f, g + o)).start()

    for o in (1, 3, 2):
        px[o - 1].wait_recv()
        share[o].start()
    px_own.wait()

    def pad(owner, counts):
        token = lax.broadcasted_iota(jnp.int32, (plen, dim), 0)

        def one(i, _):
            vectors = raw[owner, :, i].reshape(plen, dim).astype(jnp.float32)
            kept = jnp.where(token < counts[x * held + i], vectors, vectors[0:1, :])
            ps[owner, i] = kept.astype(jnp.bfloat16).reshape(ps.shape[2:])
            return 0
        lax.fori_loop(0, held, one, 0, unroll=4)

    pad(core, len_ref)
    lens_out.wait_recv()
    for copy in share:
        copy.wait_recv()
    pad(1 - core, len_far)

    maxima[...] = jnp.zeros_like(maxima)

    def line_arrived(z):
        remote(qs.at[z], qs.at[z], line_send, line_recv.at[z], sibling).wait_recv()

    def step(z, _):
        @pl.when(jnp.logical_and(core == 1, z == 0))
        def _():
            for way in (1, -1):
                far = wrap(zz - 2 * way, side)
                line_arrived(far)
                remote(qs.at[far], qs.at[far], line_send, line_recv.at[far], at(f, g + way)).start()
                part = qs.at[far, pl.ds(0 if way == 1 else side // 2, side // 2)]
                remote(part, part, line_send, line_recv.at[far], at(f, g + 2 * way)).start()

        apart = wrap(z - zz, side)

        @pl.when(jnp.logical_and(core == 1, jnp.logical_and(apart != 0, jnp.logical_and(
            apart != 2, apart != side - 2))))
        def _():
            line_arrived(z)

        @pl.when(jnp.logical_and(core == 0, z % 2 == 0))
        def _():
            pairs = qs.at[pl.ds(0, 2), pl.ds(0, side - 1)]
            remote(pairs, pairs, line_send, line_recv.at[z], sibling).wait_recv()
        before = jnp.maximum(z - 1, 0)
        last = maxima[...]
        maxima[...] = best_match(z)
        add_up(last, before)

        @pl.when(z > 0)
        def _():
            send_rows(before)
        return 0
    lax.fori_loop(0, side, step, 0)
    add_up(maxima[...], side - 1)
    send_rows(side - 1)
    table[pl.ds(2 * (me // 2), 2)] = rows[:, zz, yy]

    rest = table.at[pl.ds(0, owners - 2)]
    remote(rest, rest, row_send, row_recv, sibling).wait_recv()
    picked = jnp.take_along_axis(table[...].reshape(owners, 128), idx[...], axis=1, mode="promise_in_bounds")
    picked = picked.T[:slots, :]
    slot = lax.broadcasted_iota(jnp.int32, (slots, owners), 0)
    outs[0] = jnp.where(slot < cnt_ref[...], picked, 0.0)
    out_copies = [remote(outs.at[0], outs.at[o], out_send.at[o], out_recv.at[o], along_x(o)) for o in range(1, xs)]
    for copy in out_copies:
        copy.start()
    total = outs[0]
    for o, copy in zip(range(1, xs), out_copies):
        copy.wait_recv()
        total = total + outs[o]
    o_ref[...] = total

    for copy in out_copies + px + share + [lens_out]:
        copy.wait_send()
    blocks = qs.at[0, pl.ds(0, side - 1)]
    remote(blocks, blocks, near_send, near_recv.at[0], sibling).wait_send()
    lines = qs.at[pl.ds(0, side - 1)]
    remote(lines, lines, line_send, line_recv.at[0], sibling).wait_send()
    remote(rest, rest, row_send, row_recv, sibling).wait_send()


def local(side, xs, queries, passages, lengths, pair_query, pair_passage, send_counts):
    owners, slots = pair_query.shape
    q_dev, q_tokens, dim = queries.shape
    per_owner, block, _ = passages.shape
    held = per_owner // xs
    dma = pltpu.SemaphoreType.DMA
    out = pl.pallas_call(
        functools.partial(kernel, side, xs, q_dev),
        out_shape=jax.ShapeDtypeStruct((slots, owners), jnp.float32),
        in_specs=[pl.BlockSpec(memory_space=pltpu.HBM)] * 6,
        out_specs=pl.BlockSpec(memory_space=pltpu.VMEM),
        scratch_shapes=[
            pltpu.SMEM((per_owner,), jnp.int32),
            pltpu.SMEM((per_owner,), jnp.int32),
            pltpu.VMEM((slots, owners), jnp.int32),
            pltpu.VMEM((slots, owners), jnp.int32),
            pltpu.VMEM((1, owners), jnp.int32),
            pltpu.VMEM((side, side, q_dev * q_tokens, dim), jnp.bfloat16),
            pltpu.VMEM((2, xs, held, block, dim), jnp.bfloat16),
            pltpu.VMEM((2, held, xs, block, dim), jnp.bfloat16),
            pltpu.VMEM((2 * held, side * q_dev * q_tokens), jnp.float32),
            pltpu.VMEM((2, side, side, 1, 128), jnp.float32),
            pltpu.VMEM((owners, 1, 128), jnp.float32),
            pltpu.VMEM((owners, 128), jnp.int32),
            pltpu.VMEM((xs, slots, owners), jnp.float32),
            dma((5,)), dma, dma, dma, dma((side,)), dma, dma((side,)), dma((xs,)), dma((xs,)),
            dma((xs,)), dma((xs,)), dma, dma, dma, dma((xs,)), dma((xs,)),
        ],
        compiler_params=pltpu.CompilerParams(
            collective_id=0, has_side_effects=True, vmem_limit_bytes=60 * 2**20),
        cost_estimate=pl.CostEstimate(
            flops=2 * per_owner * block * owners * q_dev * q_tokens * dim, bytes_accessed=8 * 2**20,
            transcendentals=0),
    )(queries.reshape(q_dev * q_tokens, dim), passages, lengths,
      pair_query.T, pair_passage.T, send_counts.reshape(1, owners))
    return out.T


def solution(mesh):
    placed = (
        P("shard", None, None),
        P("shard", "blk", None),
        P("shard"),
        P("shard", None),
        P("shard", None),
        P("shard"),
    )
    side = math.isqrt(mesh.shape["shard"] // 2)
    return jax.shard_map(
        functools.partial(local, side, mesh.shape["blk"]),
        mesh=mesh, in_specs=placed, out_specs=P("shard", None), check_vma=False
    )
```

time: 49.7 us -> 45.3 us (0.911)
  the two profiles are of different devices: /device:TPU:56 before, /device:TPU:1 now
where the time goes in v3:
time: 45.3 us; the launch traced here: 45.1 us
  Pallas kernels  43.8 us (97%)
  local copies, waits for them, and re-layouts  1.3 us (3%)
    pallas_call x1, Pallas kernels, local(): pl.pallas_call(functools.partial(kernel, side, xs, q_dev), out_shape=jax....  43.8 us
    unnamed x1, local copies, waits for them, and re-layouts  1.3 us

profile of v3, /device:TPU:1, one launch (start us, length us, event | category | flops | bytes accessed | tf_op | source)
XLA Modules:
  0.0 45.1 jit_solution(17813992097875760708)
XLA Ops:
  0.0 43.8 %shard_map.64 = f32[12,128]{1,0:T(8,128)} custom-call(bf16[64,128]{1,0:T(8,128)(2,1)} %bitcast.6, bf16[64,32,128]{2,1,0:T(8,128)(2,1)} %p_hbm.1, s32[64]{0:T(128)} %len_hbm.1, s32[12,128]{1,0:T(8,128)} %bitcast.7, s32[12,128]{1,0:T(8,128)} %bitcast.8, s32[1,128]{1,0:T(1,128)} %bitcast.9), custom_call_target="tpu_custom_call" | custom-call | flops 4294967296 | bytes 8388608 | tf_op jit(solution)/shard_map/pallas_call | solution.py:242
  43.8 1.3 %copy.8 = f32[128,12]{0,1:T(8,128)} copy(f32[128,12]{0,1:T(8,128)} %bitcast.5) | data formatting | bytes 12288

commit v4 on v3

--- a/solution.py
+++ b/solution.py
@@ -13,7 +13,7 @@
 
 def kernel(side, xs, q_dev, q_hbm, p_hbm, len_hbm, pq_hbm, pp_hbm, cnt_hbm, o_ref,
            len_ref, len_far, pq_ref, pp_ref, cnt_ref, qs, raw, ps, maxima, rows, table, idx, outs,
-           in_sems, len_send, len_recv, near_send, near_recv, line_send, line_recv, sib_send, sib_recv,
+           in_sems, len_send, len_recv, near_send, near_recv, line_send, line_recv, hand_send, sib_send, sib_recv,
            px_send, px_recv, px_local, row_send, row_recv, out_send, out_recv):
     me = lax.axis_index("shard")
     x = lax.axis_index("blk")
@@ -90,10 +90,12 @@
     plen = ps.shape[2] * ps.shape[3]
     dim = ps.shape[4]
 
-    def best_match(gg):
-        sims = lax.dot_general(ps[...].reshape(2 * held * plen, dim), qs[gg].reshape(n, dim), NT,
+    def best_match(gg, c=None):
+        tokens_of = ps[...] if c is None else ps[c]
+        count = 2 * held if c is None else held
+        sims = lax.dot_general(tokens_of.reshape(count * plen, dim), qs[gg].reshape(n, dim), NT,
                                preferred_element_type=jnp.float32)
-        return jnp.max(sims.reshape(2 * held, plen, n), axis=1)
+        return jnp.max(sims.reshape(count, plen, n), axis=1)
 
     def add_up(best, gg):
         high = best.astype(jnp.bfloat16)
@@ -118,7 +120,7 @@
         return {"shard": (y * side + z) * 2 + core}
 
     def send_rows(z):
-        for o in range(1, side):
+        for o in (4, 3, 5, 2, 6, 1, 7):
             y = wrap(yy + o, side)
             remote(rows.at[:, z, y], mine, row_send, row_recv, owner_at(y, z)).start()
 
@@ -134,12 +136,12 @@
     def _():
         for o in range(1, side):
             near_arrived(wrap(f + o, side))
-        for o in (1, -1, 2, -2):
+        for o in (2, -2, 1, -1):
             remote(qs.at[zz], qs.at[zz], line_send, line_recv.at[zz], at(f, g + o)).start()
 
     @pl.when(core == 0)
     def _():
-        for z in range(0, side, 2):
+        for z in range(0, side - 2, 2):
             for ff in (z, z + 1):
                 @pl.when(ff != f)
                 def _():
@@ -148,6 +150,15 @@
             for o in (4, 3, 5, 2, 6, 1, 7):
                 remote(pair, pair, line_send, line_recv.at[z], at(f, g + o)).start()
 
+    def last_pair():
+        for ff in (side - 2, side - 1):
+            @pl.when(ff != f)
+            def _():
+                near_arrived(ff)
+        pair = qs.at[pl.ds(side - 2, 2), yy]
+        for o in (4, 3, 5, 2, 6, 1, 7):
+            remote(pair, pair, line_send, line_recv.at[side - 2], at(f, g + o)).start()
+
     for o in (1, 3, 2):
         px[o - 1].wait_recv()
         share[o].start()
@@ -163,50 +174,73 @@
             return 0
         lax.fori_loop(0, held, one, 0, unroll=4)
 
+    def line_arrived(z):
+        remote(qs.at[z], qs.at[z], line_send, line_recv.at[z], sibling).wait_recv()
+
+    def handed_on(way):
+        far = wrap(zz - 2 * way, side)
+        part = qs.at[far, pl.ds(0 if way == 1 else side // 2, side // 2)]
+        return far, [remote(qs.at[far], qs.at[far], hand_send.at[(way + 1) // 2], line_recv.at[far], at(f, g + way)),
+                     remote(part, part, hand_send.at[(way + 1) // 2], line_recv.at[far], at(f, g + 2 * way))]
+
+    hands = [handed_on(1), handed_on(-1)]
+
+    def apart(z):
+        return wrap(z - zz, side)
+
+    def key(z):
+        distant = jnp.logical_and(apart(z) > 2, apart(z) < side - 2)
+        return 4 * z + jnp.where(jnp.logical_and(core == 1, distant), (14, 11, 10, 9)[z] if z < 4 else 14, 0)
+
+    keys = [key(z) for z in range(side)]
+    ranks = [sum(jnp.where(other < mine_, 1, 0) for other in keys) for mine_ in keys]
+    order = [sum(jnp.where(rank == i, z, 0) for z, rank in enumerate(ranks)) for i in range(side)]
+
+    def fetch(i):
+        z = sum(jnp.where(i == at_, place, 0) for at_, place in enumerate(order))
+
+        got = jnp.logical_or(apart(z) == 2, apart(z) == side - 2)
+
+        @pl.when(jnp.logical_and(core == 1, jnp.logical_and(z != zz, jnp.logical_not(got))))
+        def _():
+            line_arrived(z)
+
+        @pl.when(jnp.logical_and(core == 0, z % 2 == 0))
+        def _():
+            pairs = qs.at[pl.ds(0, 2), pl.ds(0, side - 1)]
+            remote(pairs, pairs, line_send, line_recv.at[z], sibling).wait_recv()
+        return z
+
     pad(core, len_ref)
+
+    def hand_on(early):
+        for far, copies in hands:
+            @pl.when(jnp.logical_and(core == 1, (far < side // 2) == early))
+            def _():
+                line_arrived(far)
+                for copy in copies:
+                    copy.start()
+
+    hand_on(True)
+
+    first = fetch(0)
+    maxima[pl.ds(pl.multiple_of(core * held, 8), held)] = best_match(first, core)
     lens_out.wait_recv()
     for copy in share:
         copy.wait_recv()
     pad(1 - core, len_far)
-
-    maxima[...] = jnp.zeros_like(maxima)
-
-    def line_arrived(z):
-        remote(qs.at[z], qs.at[z], line_send, line_recv.at[z], sibling).wait_recv()
-
-    def step(z, _):
-        @pl.when(jnp.logical_and(core == 1, z == 0))
-        def _():
-            for way in (1, -1):
-                far = wrap(zz - 2 * way, side)
-                line_arrived(far)
-                remote(qs.at[far], qs.at[far], line_send, line_recv.at[far], at(f, g + way)).start()
-                part = qs.at[far, pl.ds(0 if way == 1 else side // 2, side // 2)]
-                remote(part, part, line_send, line_recv.at[far], at(f, g + 2 * way)).start()
-
-        apart = wrap(z - zz, side)
-
-        @pl.when(jnp.logical_and(core == 1, jnp.logical_and(apart != 0, jnp.logical_and(
-            apart != 2, apart != side - 2))))
-        def _():
-            line_arrived(z)
-
-        @pl.when(jnp.logical_and(core == 0, z % 2 == 0))
-        def _():
-            pairs = qs.at[pl.ds(0, 2), pl.ds(0, side - 1)]
-            remote(pairs, pairs, line_send, line_recv.at[z], sibling).wait_recv()
-        before = jnp.maximum(z - 1, 0)
-        last = maxima[...]
-        maxima[...] = best_match(z)
-        add_up(last, before)
-
-        @pl.when(z > 0)
-        def _():
-            send_rows(before)
+    maxima[pl.ds(pl.multiple_of((1 - core) * held, 8), held)] = best_match(first, 1 - core)
+    add_up(maxima[...], first)
+    send_rows(first)
+    pl.when(core == 0)(last_pair)
+    hand_on(False)
+
+    def step(i, _):
+        z = fetch(i)
+        add_up(best_match(z), z)
+        send_rows(z)
         return 0
-    lax.fori_loop(0, side, step, 0)
-    add_up(maxima[...], side - 1)
-    send_rows(side - 1)
+    lax.fori_loop(1, side, step, 0)
     table[pl.ds(2 * (me // 2), 2)] = rows[:, zz, yy]
 
     rest = table.at[pl.ds(0, owners - 2)]
@@ -216,8 +250,8 @@
     slot = lax.broadcasted_iota(jnp.int32, (slots, owners), 0)
     outs[0] = jnp.where(slot < cnt_ref[...], picked, 0.0)
     out_copies = [remote(outs.at[0], outs.at[o], out_send.at[o], out_recv.at[o], along_x(o)) for o in range(1, xs)]
-    for copy in out_copies:
-        copy.start()
+    for o in (2, 1, 3):
+        out_copies[o - 1].start()
     total = outs[0]
     for o, copy in zip(range(1, xs), out_copies):
         copy.wait_recv()
@@ -228,8 +262,16 @@
         copy.wait_send()
     blocks = qs.at[0, pl.ds(0, side - 1)]
     remote(blocks, blocks, near_send, near_recv.at[0], sibling).wait_send()
-    lines = qs.at[pl.ds(0, side - 1)]
-    remote(lines, lines, line_send, line_recv.at[0], sibling).wait_send()
+    for count, which in ((side - 1, core == 0), (4, core == 1)):
+        @pl.when(which)
+        def _():
+            lines = qs.at[pl.ds(0, count)]
+            remote(lines, lines, line_send, line_recv.at[0], sibling).wait_send()
+    for way in range(2):
+        @pl.when(core == 1)
+        def _():
+            amount = qs.at[pl.ds(0, 3), pl.ds(0, side // 2)]
+            remote(amount, amount, hand_send.at[1 - way], line_recv.at[0], sibling).wait_send()
     remote(rest, rest, row_send, row_recv, sibling).wait_send()
 
 
@@ -258,7 +300,7 @@
             pltpu.VMEM((owners, 1, 128), jnp.float32),
             pltpu.VMEM((owners, 128), jnp.int32),
             pltpu.VMEM((xs, slots, owners), jnp.float32),
-            dma((5,)), dma, dma, dma, dma((side,)), dma, dma((side,)), dma((xs,)), dma((xs,)),
+            dma((5,)), dma, dma, dma, dma((side,)), dma, dma((side,)), dma((2,)), dma((xs,)), dma((xs,)),
             dma((xs,)), dma((xs,)), dma, dma, dma, dma((xs,)), dma((xs,)),
         ],
         compiler_params=pltpu.CompilerParams(

time: 45.3 us -> 43.1 us (0.951)
  Pallas kernels: 43.8 us -> 41.6 us
    pallas_call x1, Pallas kernels: 43.8 us -> 41.6 us  [local(): pl.pallas_call(functools.partial(kernel, side, xs, q_dev), out_shape=jax....]
where the time goes in v4:
time: 43.1 us; the launch traced here: 42.9 us
  Pallas kernels  41.6 us (97%)
  local copies, waits for them, and re-layouts  1.3 us (3%)
    pallas_call x1, Pallas kernels, local(): pl.pallas_call(functools.partial(kernel, side, xs, q_dev), out_shape=jax....  41.6 us
    unnamed x1, local copies, waits for them, and re-layouts  1.3 us

profile of v4, /device:TPU:1, one launch (start us, length us, event | category | flops | bytes accessed | tf_op | source)
XLA Modules:
  0.0 42.9 jit_solution(7466135799339165673)
XLA Ops:
  0.0 41.6 %shard_map.64 = f32[12,128]{1,0:T(8,128)} custom-call(bf16[64,128]{1,0:T(8,128)(2,1)} %bitcast.6, bf16[64,32,128]{2,1,0:T(8,128)(2,1)} %p_hbm.1, s32[64]{0:T(128)} %len_hbm.1, s32[12,128]{1,0:T(8,128)} %bitcast.7, s32[12,128]{1,0:T(8,128)} %bitcast.8, s32[1,128]{1,0:T(1,128)} %bitcast.9), custom_call_target="tpu_custom_call" | custom-call | flops 4294967296 | bytes 8388608 | tf_op jit(solution)/shard_map/pallas_call | solution.py:284
  41.6 1.3 %copy.8 = f32[128,12]{0,1:T(8,128)} copy(f32[128,12]{0,1:T(8,128)} %bitcast.5) | data formatting | bytes 12288
